TPU v7x, 256 devices: a whole 4x4x8 slice. The times are simulated.
256 devices in a mesh: row: 16 (over z_lo, x), col: 16 (over z_hi, y, core).
Axes of the slice: x: 4, y: 4, z: 8 (z_hi: 2, z_lo: 4; z = z_hi * 4 + z_lo), core: 2. Of those that a mesh axis runs over, the one named last changes fastest.
Arguments:
- inverse_tiles: bfloat16 [16384, 16384], P('row', 'col'), may hold values from -0.046875 to 0.046875
- factor: bfloat16 [16384, 4, 512], P('row', None, 'col'), may hold values from -0.75 to 0.75
- inverse_diag: float32 [4, 512, 512], P(None, 'row', 'col'), may hold values from -6 to 6
- tile_list: int32 [4, 128], replicated, may hold values from 0 to 127, as said below
- tile_count: int32 [4], replicated, may hold values from 86 to 128, as said below
Outputs:
- inverse_panel: bfloat16 [16384, 4, 512], P(('row', 'col'))
- diag_block: float32 [4, 512, 512], P(None, 'row', 'col')
Inputs may be any that keep to these rules, and one draw needn't show every extreme that they name: For each supernode the first tile_count entries of tile_list name distinct tiles in increasing order; the remaining entries name the tiles that are not listed. `tile_count`: some supernode lists all 128 tiles.
All inputs are finite; a program needn't handle non-finite values.
Results may differ from a plain program's by a relative error of at most 0.014.
Values may be sent and summed in bfloat16 or wider, within the bound.
A program may use at most 64 MiB of HBM per device.

v0:
```python
import jax
import jax.numpy as jnp
from jax import lax
from jax.sharding import Mesh
from jax.sharding import PartitionSpec as P

TILE = 128
COL = ("col_0", "col_1", "col_2")
ROW_COL = ("row", "col_0", "col_1", "col_2")


def spread(x, axis, root):
    mine = lax.axis_index(axis) == root
    return lax.psum(jnp.where(mine, x, jnp.zeros_like(x)), axis)


def split_up(x, dim, size):
    before, after = (x.shape[:dim], x.shape[dim + 1 :])
    return jnp.moveaxis(x.reshape(*before, size, -1, *after), dim, 0)


def summed_rows(x, chips, core, dim):
    sizes = (lax.axis_size(chips), lax.axis_size(core))
    blocks = split_up(x, dim, sizes[0] * sizes[1])
    inside = blocks.shape[1:]
    blocks = blocks.reshape(*sizes, *inside).swapaxes(0, 1).reshape(-1, *inside)
    blocks = lax.psum_scatter(blocks, core, scatter_dimension=0, tiled=True)
    return lax.psum_scatter(blocks, chips, scatter_dimension=0, tiled=True)[0]


def sent_and_summed(x, axis, dim):
    blocks = split_up(x, dim, lax.axis_size(axis))
    arrived = lax.all_to_all(blocks, axis, split_axis=0, concat_axis=0, tiled=True)
    return arrived.astype(jnp.float32).sum(axis=0)


def per_device(inverse_tiles, factor, inverse_diag, tile_list, tile_count):
    row_devices = lax.axis_size("row")
    col_devices = lax.axis_size(COL)
    row_index = lax.axis_index("row")
    col_index = lax.axis_index(COL)
    rows_blk = inverse_tiles.shape[0]
    cols_blk = inverse_tiles.shape[1]
    supers = factor.shape[1]
    panel_width = factor.shape[2] * col_devices
    tile_total = tile_list.shape[1]
    position = jnp.arange(tile_total, dtype=jnp.int32)
    matches = (tile_list[:, :, None] == position[None, None, :]) & (
        position[None, :, None] < tile_count[:, None, None]
    )
    listed = jnp.any(matches, axis=1).astype(jnp.float32)
    live_all = jnp.repeat(listed, TILE, axis=1)
    row_live = lax.dynamic_slice_in_dim(live_all, row_index * rows_blk, rows_blk, 1).T
    row_factor = lax.all_gather(factor, COL, axis=2, tiled=True)
    row_factor = jnp.where(row_live[:, :, None] > 0, row_factor, jnp.zeros_like(row_factor))
    blocks_per = row_devices // col_devices
    received = spread(row_factor, "row", col_index * blocks_per + 0)
    col_factor = received.reshape(cols_blk, supers * panel_width)
    whole_term = jnp.dot(inverse_tiles, col_factor, preferred_element_type=jnp.float32).reshape(
        rows_blk, supers, panel_width
    )
    panel_cols = summed_rows(whole_term, ("col_0", "col_1"), "col_2", 2)
    panel_cols = -panel_cols * row_live[:, :, None]
    diag_part = jnp.einsum(
        "rsv,rsw->svw", row_factor.astype(jnp.float32), panel_cols, precision=lax.Precision.HIGHEST
    )
    diag_mine = sent_and_summed(diag_part.astype(jnp.bfloat16), "row", 1)
    inverse_panel = lax.all_to_all(
        panel_cols.astype(jnp.bfloat16), COL, split_axis=0, concat_axis=2, tiled=True
    )
    diag_block = inverse_diag - diag_mine
    return (inverse_panel, diag_block)


def solution(mesh):
    torus = Mesh(
        mesh.devices.reshape(mesh.shape["row"], 2, 4, 2), ("row", "col_0", "col_1", "col_2")
    )
    return jax.shard_map(
        per_device,
        mesh=torus,
        in_specs=(P("row", COL), P("row", None, COL), P(None, "row", COL), P(), P()),
        out_specs=(P(ROW_COL, None, None), P(None, "row", COL)),
        check_vma=False,
    )
```

profile of v0, /device:TPU:32, one launch (start us, length us, event | category | flops | bytes accessed | tf_op | source)
XLA Modules:
  0.0 482.2 jit_solution(6248333700501249892)
XLA Ops:
  7.2 0.0 copy-start
  7.2 0.0 all-gather.2.cloned.1.call-start
  7.2 0.7 all-gather.2.cloned.1.call-update
  7.9 0.0 all-reduce.2.cloned.1.call-start
  8.0 0.7 iota_compare_fusion.1
  8.7 0.9 fusion.6
  9.6 0.1 broadcast_bitcast_fusion
  9.7 0.2 copy.57
  9.9 79.6 %all-gather.2.cloned.1.call-done = bf16[1024,4,512]{0,2,1:T(8,128)(2,1)} async-done(((bf16[1024,4,32]{0,2,1:T(8,128)(2,1)}), bf16[1024,4,512]{0,2,1:T(8,128)(2,1)}) %all-gather.2.cloned.1.call-update) | async-done | bytes 4194320 | tf_op jit(solution)/shard_map/all_gather | solution.py:54
  89.5 4.5 broadcast_select_fusion.1
  94.1 0.0 all-reduce.2.cloned.1.call-update
  94.1 0.0 reduce-scatter.3.cloned.1.call-start
  94.1 169.6 %all-reduce.2.cloned.1.call-done = bf16[1024,2048]{0,1:T(8,128)(2,1)} async-done(((bf16[1024,2048]{0,1:T(8,128)(2,1)}), bf16[1024,2048]{0,1:T(8,128)(2,1)}) %all-reduce.2.cloned.1.call-update) | async-done | bytes 4194320 | tf_op jit(solution)/shard_map/psum | solution.py:14
  263.7 0.0 copy-done
  263.7 6.4 %fusion.9 = f32[2048,1024]{1,0:T(8,128)S(1)} fusion(bf16[1024,2048]{0,1:T(8,128)(2,1)} %all-reduce.2.cloned.1.call-done, bf16[1024,1024]{1,0:T(8,128)(2,1)S(1)} %copy-done), kind=kOutput, calls=%fused_computation.20 | convolution fusion | flops 4294967296 | bytes 14680064 | tf_op jit(solution)/shard_map/dot_general | solution.py:59
  270.1 4.1 copy.38
  274.2 0.0 reduce-scatter.3.cloned.1.call-update
  274.2 0.0 reduce-scatter.5.cloned.1.call-start
  274.3 25.8 %reduce-scatter.3.cloned.1.call-done = f32[8,1024,4,32]{1,3,2,0:T(8,128)} async-done(((f32[16,1024,4,32]{1,3,2,0:T(8,128)}), f32[8,1024,4,32]{1,3,2,0:T(8,128)}) %reduce-scatter.3.cloned.1.call-update) | async-done | bytes 4194320 | tf_op jit(solution)/shard_map/reduce_scatter | solution.py:27
  300.1 0.0 reduce-scatter.5.cloned.1.call-update
  300.1 131.2 %reduce-scatter.5.cloned.1.call-done = f32[1,1024,4,32]{1,3,2,0:T(8,128)} async-done(((f32[8,1024,4,32]{1,3,2,0:T(8,128)}), f32[1,1024,4,32]{1,3,2,0:T(8,128)}) %reduce-scatter.5.cloned.1.call-update) | async-done | bytes 524304 | tf_op jit(solution)/shard_map/reduce_scatter | solution.py:28
  431.3 6.0 %fusion.2 = bf16[4,512,32]{1,2,0:T(8,128)(2,1)S(1)} fusion(bf16[1024,4,512]{0,2,1:T(8,128)(2,1)} %all-gather.2.cloned.1.call-done, pred[1024,4]{0,1:T(4,128)(4,1)S(1)} %get-tuple-element.12, f32[1,1024,4,32]{1,3,2,0:T(8,128)} %reduce-scatter.5.cloned.1.call-done, f32[1024,4]{0,1:T(4,128)S(1)} %get-tuple-element.13), kind=kOutput, calls=%fused_computation.4 | convolution fusion | flops 807731200 | bytes 4870144 | tf_op jit(solution)/shard_map/rsv,rsw->svw/dot_general | solution.py:64
  437.3 0.3 reshape.53
  437.6 0.1 copy.58
  437.7 1.2 reshape.56
  438.9 5.8 %all-to-all-start.1 = ((bf16[16,2,2048]{2,1,0:T(2,128)(2,1)}), bf16[16,2,2048]{2,1,0:T(2,128)(2,1)S(1)}, u32[]{:S(2)}, u32[]{:S(2)}) async-start(bf16[16,2,2048]{2,1,0:T(2,128)(2,1)} %reshape.56), calls=%async_computation.3 | async-start | bytes 262144 | tf_op jit(solution)/shard_map/all_to_all | solution.py:33
  444.7 1.1 fusion.3
  445.8 0.7 copy.39
  446.5 1.7 reshape.54
  448.2 3.4 all-to-all-done.1
  451.6 5.4 %all-to-all-start = ((bf16[16,2,4096]{2,1,0:T(2,128)(2,1)}), bf16[16,2,4096]{2,1,0:T(2,128)(2,1)S(1)}, u32[]{:S(2)}, u32[]{:S(2)}) async-start(bf16[16,2,4096]{2,1,0:T(2,128)(2,1)} %reshape.54), calls=%async_computation.2 | async-start | bytes 524288 | tf_op jit(solution)/shard_map/all_to_all | solution.py:68
  457.0 0.9 copy.45
  457.9 0.3 reshape.57
  458.2 0.1 convert_reduce_fusion
  458.3 0.7 copy.47
  459.1 12.7 %all-to-all-done = bf16[16,2,4096]{2,1,0:T(2,128)(2,1)S(1)} async-done(((bf16[16,2,4096]{2,1,0:T(2,128)(2,1)}), bf16[16,2,4096]{2,1,0:T(2,128)(2,1)S(1)}, u32[]{:S(2)}, u32[]{:S(2)}) %all-to-all-start) | async-done | bytes 262176 | tf_op jit(solution)/shard_map/all_to_all | solution.py:68
  471.8 0.5 reshape.55
  472.3 1.3 copy.50
  473.6 2.0 copy.46
  (3 shorter events, 0.0 us)
Async XLA Ops:
  7.2 256.6 %copy-start = (bf16[1024,1024]{1,0:T(8,128)(2,1)S(1)}, bf16[1024,1024]{1,0:T(8,128)(2,1)}, u32[]{:S(2)}) copy-start(bf16[1024,1024]{1,0:T(8,128)(2,1)} %param.5) | copy-start | bytes 6291460
  7.2 82.4 %all-gather.2.cloned.1.call-start = ((), (), s32[]{:S(2)}) async-start(), calls=%async_computation.4 | async-start | bytes 4456448 | tf_op jit(solution)/shard_map/all_gather | solution.py:54
  7.9 255.8 %all-reduce.2.cloned.1.call-start = ((), (), s32[]{:S(2)}) async-start(), calls=%async_computation.5 | async-start | bytes 8388608 | tf_op jit(solution)/shard_map/psum | solution.py:14
  94.1 206.0 %reduce-scatter.3.cloned.1.call-start = ((), (), s32[]{:S(2)}) async-start(), calls=%async_computation.6 | async-start | bytes 12582912 | tf_op jit(solution)/shard_map/reduce_scatter | solution.py:27
  274.2 157.1 %reduce-scatter.5.cloned.1.call-start = ((), (), s32[]{:S(2)}) async-start(), calls=%async_computation.7 | async-start | bytes 4718592 | tf_op jit(solution)/shard_map/reduce_scatter | solution.py:28
  438.9 12.7 %all-to-all-start.1 = ((bf16[16,2,2048]{2,1,0:T(2,128)(2,1)}), bf16[16,2,2048]{2,1,0:T(2,128)(2,1)S(1)}, u32[]{:S(2)}, u32[]{:S(2)}) async-start(bf16[16,2,2048]{2,1,0:T(2,128)(2,1)} %reshape.56), calls=%async_computation.3 | async-start | bytes 262144 | tf_op jit(solution)/shard_map/all_to_all | solution.py:33
  451.6 20.2 %all-to-all-start = ((bf16[16,2,4096]{2,1,0:T(2,128)(2,1)}), bf16[16,2,4096]{2,1,0:T(2,128)(2,1)S(1)}, u32[]{:S(2)}, u32[]{:S(2)}) async-start(bf16[16,2,4096]{2,1,0:T(2,128)(2,1)} %reshape.54), calls=%async_computation.2 | async-start | bytes 524288 | tf_op jit(solution)/shard_map/all_to_all | solution.py:68
Sparse Core Ops, SparseCore 0:
  10.8 78.7 all-gather.1
  94.2 169.4 all-reduce.1
  274.3 25.6 reduce-scatter.2
  304.6 126.5 reduce-scatter.4
where the time goes:
time: 483 us; the launch traced here: 482 us
  waiting for transfers between devices  423 us (88%)
  local copies, waits for them, and re-layouts  14.1 us (3%)
  between operations  13.9 us (3%)
  matrix products  12.3 us (3%)
  starting transfers between devices  11.4 us (2%)
  other arithmetic  7.39 us (2%)
    psum x1, waiting for transfers between devices, spread(): return lax.psum(jnp.where(mine, x, jnp.zeros_like(x)), axis)  170 us
    reduce_scatter x1, waiting for transfers between devices, summed_rows(): return lax.psum_scatter(blocks, chips, scatter_dimension=0, tiled=True)[0]  131 us
    all_gather x1, waiting for transfers between devices, per_device(): row_factor = lax.all_gather(factor, COL, axis=2, tiled=True)  79.6 us
    reduce_scatter x1, waiting for transfers between devices, summed_rows(): blocks = lax.psum_scatter(blocks, core, scatter_dimension=0, tiled=True)  25.8 us
    all_to_all x1, waiting for transfers between devices, per_device(): lax.all_to_all(panel_cols.astype(jnp.bfloat16), COL, split_axis=0, concat...  12.7 us
  transfers between devices with their start and end apart: 6, of which 6 were waited for; matrix products, arithmetic and copies ran while one was open for 2% of the time, Pallas kernels for 0%

commit v1 on v0

--- a/solution.py
+++ b/solution.py
@@ -51,7 +51,11 @@
     listed = jnp.any(matches, axis=1).astype(jnp.float32)
     live_all = jnp.repeat(listed, TILE, axis=1)
     row_live = lax.dynamic_slice_in_dim(live_all, row_index * rows_blk, rows_blk, 1).T
-    row_factor = lax.all_gather(factor, COL, axis=2, tiled=True)
+    find_vectors = lambda shard_in, mesh_ax: jnp.concatenate(
+        lax.all_to_all(jnp.stack([shard_in for _ in range(lax.axis_size(mesh_ax))]), mesh_ax, 0, 0),
+        2,
+    )
+    row_factor = find_vectors(factor, COL)
     row_factor = jnp.where(row_live[:, :, None] > 0, row_factor, jnp.zeros_like(row_factor))
     blocks_per = row_devices // col_devices
     received = spread(row_factor, "row", col_index * blocks_per + 0)

time: 483 us -> 526 us (1.089)
  waiting for transfers between devices: 423 us -> 450 us
  starting transfers between devices: 11.4 us -> 21.8 us
  local copies, waits for them, and re-layouts: 14.1 us -> 22.3 us
    all_to_all x0 -> x1, waiting for transfers between devices: none -> 98.4 us  [per_device(): lax.all_to_all(jnp.stack([shard_in for _ in range(lax.axis_size(mesh_ax))...]
    all_gather x1 -> x0, waiting for transfers between devices: 79.6 us -> none  [per_device(): row_factor = lax.all_gather(factor, COL, axis=2, tiled=True)]
    all_to_all x0 -> x1, starting transfers between devices: none -> 10.5 us  [per_device(): lax.all_to_all(jnp.stack([shard_in for _ in range(lax.axis_size(mesh_ax))...]
    psum x1, waiting for transfers between devices: 170 us -> 177 us  [spread(): return lax.psum(jnp.where(mine, x, jnp.zeros_like(x)), axis)]
  transfers between devices with their start and end apart: 6 -> 6, of which waited for: 6 -> 6; matrix products, arithmetic and copies ran while one was open for 2% -> 1% of each run, Pallas kernels for 0% -> 0%
where the time goes in v1:
time: 526 us; the launch traced here: 525 us
  waiting for transfers between devices  450 us (86%)
  local copies, waits for them, and re-layouts  22.3 us (4%)
  starting transfers between devices  21.8 us (4%)
  between operations  13.9 us (3%)
  matrix products  12.4 us (2%)
    psum x1, waiting for transfers between devices, spread(): return lax.psum(jnp.where(mine, x, jnp.zeros_like(x)), axis)  177 us
    reduce_scatter x1, waiting for transfers between devices, summed_rows(): return lax.psum_scatter(blocks, chips, scatter_dimension=0, tiled=True)[0]  131 us
    all_to_all x1, waiting for transfers between devices, per_device(): lax.all_to_all(jnp.stack([shard_in for _ in range(lax.axis_size(mesh_ax))...  98.4 us
    reduce_scatter x1, waiting for transfers between devices, summed_rows(): blocks = lax.psum_scatter(blocks, core, scatter_dimension=0, tiled=True)  25.8 us
    all_to_all x1, waiting for transfers between devices, per_device(): lax.all_to_all(panel_cols.astype(jnp.bfloat16), COL, split_axis=0, concat...  12.7 us
  transfers between devices with their start and end apart: 6, of which 6 were waited for; matrix products, arithmetic and copies ran while one was open for 1% of the time, Pallas kernels for 0%

profile of v1, /device:TPU:32, one launch (start us, length us, event | category | flops | bytes accessed | tf_op | source)
XLA Modules:
  0.0 525.2 jit_solution(12575848480808284486)
XLA Ops:
  7.2 0.0 copy-start
  7.2 3.6 stack.2
  10.8 0.0 copy-start.3
  10.8 0.0 copy-start.2
  10.8 10.5 %all-to-all-start = ((bf16[16,1024,4,32]{1,3,2,0:T(8,128)(2,1)}), bf16[16,1024,4,32]{1,3,2,0:T(8,128)(2,1)}, u32[]{:S(2)}, u32[]{:S(2)}) async-start(bf16[16,1024,4,32]{1,3,2,0:T(8,128)(2,1)} %stack.2), calls=%async_computation | async-start | bytes 8388608 | tf_op jit(solution)/shard_map/all_to_all | solution.py:55
  21.3 0.0 all-reduce.2.cloned.1.call-start
  21.3 0.0 copy-done.3
  21.3 0.1 iota_compare_fusion.1
  21.4 0.0 copy-done.2
  21.4 0.2 fusion.3
  21.7 0.1 broadcast_bitcast_fusion
  21.8 0.2 copy.60
  22.0 98.4 %all-to-all-done = bf16[16,1024,4,32]{1,3,2,0:T(8,128)(2,1)} async-done(((bf16[16,1024,4,32]{1,3,2,0:T(8,128)(2,1)}), bf16[16,1024,4,32]{1,3,2,0:T(8,128)(2,1)}, u32[]{:S(2)}, u32[]{:S(2)}) %all-to-all-start) | async-done | bytes 4194336 | tf_op jit(solution)/shard_map/all_to_all | solution.py:55
  120.4 2.7 copy.40
  123.2 4.0 broadcast_select_fusion
  127.2 0.0 all-reduce.2.cloned.1.call-update
  127.2 0.0 reduce-scatter.3.cloned.1.call-start
  127.3 177.4 %all-reduce.2.cloned.1.call-done = bf16[1024,2048]{0,1:T(8,128)(2,1)} async-done(((bf16[1024,2048]{0,1:T(8,128)(2,1)}), bf16[1024,2048]{0,1:T(8,128)(2,1)}) %all-reduce.2.cloned.1.call-update) | async-done | bytes 4194320 | tf_op jit(solution)/shard_map/psum | solution.py:14
  304.7 0.0 copy-done
  304.7 6.4 %fusion.5 = f32[2048,1024]{1,0:T(8,128)S(1)} fusion(bf16[1024,2048]{0,1:T(8,128)(2,1)} %all-reduce.2.cloned.1.call-done, bf16[1024,1024]{1,0:T(8,128)(2,1)S(1)} %copy-done), kind=kOutput, calls=%fused_computation.17 | convolution fusion | flops 4294967296 | bytes 14680064 | tf_op jit(solution)/shard_map/dot_general | solution.py:63
  311.0 4.1 copy.41
  315.1 0.0 reduce-scatter.3.cloned.1.call-update
  315.1 0.0 reduce-scatter.5.cloned.1.call-start
  315.2 25.8 %reduce-scatter.3.cloned.1.call-done = f32[8,1024,4,32]{1,3,2,0:T(8,128)} async-done(((f32[16,1024,4,32]{1,3,2,0:T(8,128)}), f32[8,1024,4,32]{1,3,2,0:T(8,128)}) %reduce-scatter.3.cloned.1.call-update) | async-done | bytes 4194320 | tf_op jit(solution)/shard_map/reduce_scatter | solution.py:27
  340.9 0.0 reduce-scatter.5.cloned.1.call-update
  341.0 131.5 %reduce-scatter.5.cloned.1.call-done = f32[1,1024,4,32]{1,3,2,0:T(8,128)} async-done(((f32[8,1024,4,32]{1,3,2,0:T(8,128)}), f32[1,1024,4,32]{1,3,2,0:T(8,128)}) %reduce-scatter.5.cloned.1.call-update) | async-done | bytes 524304 | tf_op jit(solution)/shard_map/reduce_scatter | solution.py:28
  472.5 0.0 copy-start.1
  472.5 6.1 %convolution_convert_fusion = bf16[4,512,32]{1,2,0:T(8,128)(2,1)S(1)} fusion(bf16[1024,4,512]{0,2,1:T(8,128)(2,1)} %get-tuple-element.13, f32[1,1024,4,32]{1,3,2,0:T(8,128)} %reduce-scatter.5.cloned.1.call-done, f32[1024,4]{0,1:T(4,128)S(1)} %get-tuple-element.15), kind=kOutput, calls=%fused_computation.2 | convolution fusion | flops 805634048 | bytes 4866048 | tf_op jit(solution)/shard_map/rsv,rsw->svw/dot_general | solution.py:68
  478.5 0.3 reshape.63
  478.8 0.9 copy.61
  479.7 2.2 reshape.66
  482.0 5.8 %all-to-all-start.2 = ((bf16[16,2,2048]{2,1,0:T(2,128)(2,1)}), bf16[16,2,2048]{2,1,0:T(2,128)(2,1)S(1)}, u32[]{:S(2)}, u32[]{:S(2)}) async-start(bf16[16,2,2048]{2,1,0:T(2,128)(2,1)} %reshape.66), calls=%async_computation.4 | async-start | bytes 262144 | tf_op jit(solution)/shard_map/all_to_all | solution.py:33
  487.7 0.0 copy-done.1
  487.7 0.1 fusion
  487.8 0.7 copy.42
  488.5 1.7 reshape.64
  490.2 4.4 all-to-all-done.2
  494.7 5.4 %all-to-all-start.1 = ((bf16[16,2,4096]{2,1,0:T(2,128)(2,1)}), bf16[16,2,4096]{2,1,0:T(2,128)(2,1)S(1)}, u32[]{:S(2)}, u32[]{:S(2)}) async-start(bf16[16,2,4096]{2,1,0:T(2,128)(2,1)} %reshape.64), calls=%async_computation.3 | async-start | bytes 524288 | tf_op jit(solution)/shard_map/all_to_all | solution.py:72
  500.1 0.9 copy.48
  501.0 0.3 reshape.67
  501.3 0.1 convert_reduce_fusion
  501.4 0.7 copy.50
  502.1 12.7 %all-to-all-done.1 = bf16[16,2,4096]{2,1,0:T(2,128)(2,1)S(1)} async-done(((bf16[16,2,4096]{2,1,0:T(2,128)(2,1)}), bf16[16,2,4096]{2,1,0:T(2,128)(2,1)S(1)}, u32[]{:S(2)}, u32[]{:S(2)}) %all-to-all-start.1) | async-done | bytes 262176 | tf_op jit(solution)/shard_map/all_to_all | solution.py:72
  514.8 0.5 reshape.65
  515.3 1.3 copy.53
  516.7 2.0 copy.49
  (3 shorter events, 0.0 us)
Async XLA Ops:
  7.2 297.5 %copy-start = (bf16[1024,1024]{1,0:T(8,128)(2,1)S(1)}, bf16[1024,1024]{1,0:T(8,128)(2,1)}, u32[]{:S(2)}) copy-start(bf16[1024,1024]{1,0:T(8,128)(2,1)} %param.5) | copy-start | bytes 6291460
  10.8 10.6 %copy-start.3 = (s32[4]{0:T(128)S(1)}, s32[4]{0:T(128)}, u32[]{:S(2)}) copy-start(s32[4]{0:T(128)} %param.9) | copy-start | bytes 52
  10.8 10.6 %copy-start.2 = (s32[4,128]{1,0:T(4,128)S(1)}, s32[4,128]{1,0:T(4,128)}, u32[]{:S(2)}) copy-start(s32[4,128]{1,0:T(4,128)} %param.8) | copy-start | bytes 6148
  10.8 109.7 %all-to-all-start = ((bf16[16,1024,4,32]{1,3,2,0:T(8,128)(2,1)}), bf16[16,1024,4,32]{1,3,2,0:T(8,128)(2,1)}, u32[]{:S(2)}, u32[]{:S(2)}) async-start(bf16[16,1024,4,32]{1,3,2,0:T(8,128)(2,1)} %stack.2), calls=%async_computation | async-start | bytes 8388608 | tf_op jit(solution)/shard_map/all_to_all | solution.py:55
  21.3 283.4 %all-reduce.2.cloned.1.call-start = ((), (), s32[]{:S(2)}) async-start(), calls=%async_computation.5 | async-start | bytes 8388608 | tf_op jit(solution)/shard_map/psum | solution.py:14
  127.2 213.7 %reduce-scatter.3.cloned.1.call-start = ((), (), s32[]{:S(2)}) async-start(), calls=%async_computation.6 | async-start | bytes 12582912 | tf_op jit(solution)/shard_map/reduce_scatter | solution.py:27
  315.1 157.3 %reduce-scatter.5.cloned.1.call-start = ((), (), s32[]{:S(2)}) async-start(), calls=%async_computation.7 | async-start | bytes 4718592 | tf_op jit(solution)/shard_map/reduce_scatter | solution.py:28
  472.5 15.3 %copy-start.1 = (f32[1,1024,4,32]{1,3,2,0:T(8,128)S(1)}, f32[1,1024,4,32]{1,3,2,0:T(8,128)}, u32[]{:S(2)}) copy-start(f32[1,1024,4,32]{1,3,2,0:T(8,128)} %reduce-scatter.5.cloned.1.call-done) | copy-start | bytes 1572868
  482.0 12.7 %all-to-all-start.2 = ((bf16[16,2,2048]{2,1,0:T(2,128)(2,1)}), bf16[16,2,2048]{2,1,0:T(2,128)(2,1)S(1)}, u32[]{:S(2)}, u32[]{:S(2)}) async-start(bf16[16,2,2048]{2,1,0:T(2,128)(2,1)} %reshape.66), calls=%async_computation.4 | async-start | bytes 262144 | tf_op jit(solution)/shard_map/all_to_all | solution.py:33
  494.7 20.2 %all-to-all-start.1 = ((bf16[16,2,4096]{2,1,0:T(2,128)(2,1)}), bf16[16,2,4096]{2,1,0:T(2,128)(2,1)S(1)}, u32[]{:S(2)}, u32[]{:S(2)}) async-start(bf16[16,2,4096]{2,1,0:T(2,128)(2,1)} %reshape.64), calls=%async_computation.3 | async-start | bytes 524288 | tf_op jit(solution)/shard_map/all_to_all | solution.py:72
Sparse Core Ops, SparseCore 0:
  127.3 177.2 all-reduce.1
  315.2 25.6 reduce-scatter.2
  345.7 126.7 reduce-scatter.4
